TPU v7x, 256 devices: a whole 4x4x8 slice. The times are simulated.
256 devices in a mesh: expert: 32 (over z_lo, x, core), node: 8 (over y, z_hi).
Axes of the slice: x: 4, y: 4, z: 8 (z_hi: 2, z_lo: 4; z = z_hi * 4 + z_lo), core: 2. Of those that a mesh axis runs over, the one named last changes fastest.
Arguments:
- queries: bfloat16 [32, 32, 73728], P('expert', 'node'), may hold values from -48 to 48
- latent: bfloat16 [32, 2048, 576], P('expert', 'node'), may hold values from -6 to 6
- tile_mask: int32 [32, 8, 8], P('expert'), may hold values from 0 to 1, as said below
- hidden: bfloat16 [32, 32, 7168], P('expert', 'node'), may hold values from -6 to 6
- value_up: bfloat16 [128, 512, 128], P('node', 'expert'), may hold values from -0.25 to 0.25
- out_proj: bfloat16 [16384, 7168], P('node', 'expert'), may hold values from -0.375 to 0.375
- norm_gain: bfloat16 [7168], replicated, may hold values from 0.25 to 1.75
- route_ids: int32 [32, 32, 8], P('expert', 'node'), may hold values from 0 to 31, all different within a row; in each aligned block of 4 rows (0 to 3, 4 to 7, ..., all dimensions but the last counted through in order) at most 2 rows name the same one
- route_gates: float32 [32, 32, 8], P('expert', 'node'), may hold values from 0.05 to 0.6
- expert_in: bfloat16 [32, 7168, 2, 2048], P('expert', None, None, 'node'), may hold values from -0.0625 to 0.0625
- expert_out: bfloat16 [32, 2048, 7168], P('expert', 'node'), may hold values from -0.125 to 0.125
Outputs:
- latent_out: bfloat16 [32, 32, 65536], P('expert', 'node')
- attended: bfloat16 [32, 32, 7168], P('expert', 'node')
- moe_out: bfloat16 [32, 32, 7168], P('expert', 'node')
Inputs may be any that keep to these rules, and one draw needn't show every extreme that they name: `route_ids`: each token names 8 different experts; tokens are counted in sequence order, and in each aligned block of 4 tokens no expert is named more than 2 times. `tile_mask`: 1 on the diagonal of each sequence's table and 0 above it.
All inputs are finite; a program needn't handle non-finite values.
Results may differ from a plain program's by a relative error of at most 0.033.
Values may be sent and summed in bfloat16 or wider, within the bound.
No kernel may reach another device: no remote copies, remote signals or barrier semaphores. Data moves between devices by JAX's collectives and lax.ppermute only.
A program may use at most 128 MiB of HBM per device.

v0:
```python
import jax
import jax.numpy as jnp
from jax import lax
from jax.sharding import PartitionSpec as P

HEADS = 128
LAT = 512
ROPE = 64
VDIM = 128
TOP = 8
BLK = 256
QROWS = 4


score_scale = 192.0 ** (-0.5)


def slot_positions(route_table, experts, capacity):
    hits = (route_table[:, :, None] == jnp.arange(experts, dtype=jnp.int32)[None, None, :]).astype(
        jnp.int32
    )
    flat = hits.reshape(-1, experts)
    earlier = jnp.cumsum(flat, axis=0) - flat
    slot = jnp.sum(earlier * flat, axis=1).reshape(route_table.shape)
    return route_table * capacity + slot


def place_rows(token_rows, positions, slots):
    chosen = jnp.any(
        jnp.arange(slots, dtype=jnp.int32)[:, None, None] == positions[None, :, :], axis=2
    )
    return jnp.dot(
        chosen.astype(jnp.bfloat16), token_rows, preferred_element_type=jnp.float32
    ).astype(jnp.bfloat16)


def combine_rows(gate_table, positions, slots, returned):
    matches = positions[:, :, None] == jnp.arange(slots, dtype=jnp.int32)[None, None, :]
    mixing = jnp.sum(jnp.where(matches, gate_table[:, :, None], 0.0), axis=1)
    return jnp.dot(mixing, returned, precision=lax.Precision.HIGHEST)


def run_expert(received, expert_in, expert_out):
    model_width = received.shape[-1]
    flat = received.reshape(-1, model_width)
    both = jnp.dot(flat, expert_in[0].reshape(model_width, -1), preferred_element_type=jnp.float32)
    half = both.shape[1] // 2
    act = (jax.nn.silu(both[:, :half]) * both[:, half:]).astype(jnp.bfloat16)
    return (
        jnp.dot(act, expert_out[0], preferred_element_type=jnp.float32)
        .astype(jnp.bfloat16)
        .reshape(received.shape)
    )


def shards(
    queries,
    latent,
    tile_mask,
    hidden,
    value_up,
    out_proj,
    norm_gain,
    route_ids,
    route_gates,
    expert_in,
    expert_out,
):
    width = LAT + ROPE
    node_pos = lax.axis_index("node")
    node_count = lax.axis_size("node")
    expert_count = lax.axis_size("expert")
    q_tokens = queries.shape[1]
    blocks_here = q_tokens // QROWS
    row_count = q_tokens * HEADS
    n_blocks = tile_mask.shape[1]
    q_rows = queries[0].reshape(row_count, width)
    token_ids = jnp.arange(q_tokens, dtype=jnp.int32)
    q_position = (
        (node_pos * blocks_here + token_ids // QROWS) * BLK + BLK - QROWS + token_ids % QROWS
    )
    block_rows = lax.dynamic_slice_in_dim(
        tile_mask[0], node_pos * blocks_here, blocks_here, 0
    ).astype(jnp.float32)
    best = jnp.full((row_count,), -1e30, jnp.float32)
    keys = lax.all_gather(latent, "node", axis=1, tiled=True)[0]
    count = keys.shape[0]
    k_position = jnp.arange(count, dtype=jnp.int32)
    onehot_block = (
        jnp.arange(n_blocks, dtype=jnp.int32)[:, None] == (k_position // BLK)[None, :]
    ).astype(jnp.float32)
    block_ok = jnp.dot(block_rows, onehot_block) > 0.5
    causal = k_position[None, :] <= q_position[:, None]
    allowed = causal.reshape(blocks_here, QROWS, count) & block_ok[:, None, :]
    allowed = jnp.broadcast_to(allowed[:, :, None, :], (blocks_here, QROWS, HEADS, count)).reshape(
        row_count, count
    )
    scores = jnp.dot(q_rows, keys.T, preferred_element_type=jnp.float32) * score_scale
    masked = jnp.where(allowed, scores, -1e30)
    fresh = jnp.maximum(best, jnp.max(masked, axis=1))
    weights = jnp.where(allowed, jnp.exp(masked - fresh[:, None]), 0.0)
    total = jnp.sum(weights, axis=1)
    summed = jnp.dot(
        weights.astype(jnp.bfloat16), keys[:, :LAT], preferred_element_type=jnp.float32
    )
    best, total, summed = (fresh, total, summed)
    latent_rows = (summed / total[:, None]).astype(jnp.bfloat16).reshape(q_tokens, HEADS * LAT)
    latent_out = latent_rows.reshape(1, q_tokens, HEADS * LAT)
    heads_here = HEADS // node_count
    split_heads = latent_rows.reshape(q_tokens, node_count, heads_here * LAT)
    swapped = lax.all_to_all(split_heads, "node", split_axis=1, concat_axis=0, tiled=True)
    seq_tokens = swapped.shape[0]
    by_head = swapped.reshape(seq_tokens, heads_here, LAT)
    lifted = jnp.einsum(
        "thl,hlv->thv",
        by_head,
        lax.all_gather(value_up, "expert", axis=1, tiled=True),
        preferred_element_type=jnp.float32,
    )
    head_vals = lifted.astype(jnp.bfloat16).reshape(seq_tokens, heads_here * VDIM)
    partial_cols = jnp.dot(
        lax.all_gather(head_vals, "expert", axis=0, tiled=True),
        out_proj,
        preferred_element_type=jnp.float32,
    )
    col_count = out_proj.shape[1]
    regrouped = partial_cols.reshape(expert_count, node_count, q_tokens, col_count).transpose(
        1, 0, 2, 3
    )
    regrouped = regrouped.reshape(node_count, expert_count * q_tokens, col_count)
    head_total = lax.psum_scatter(
        regrouped.astype(jnp.bfloat16), "node", scatter_dimension=0, tiled=True
    ).astype(jnp.float32)
    own_columns = head_total.reshape(expert_count, q_tokens, col_count)
    projected = (
        lax.all_to_all(
            own_columns.astype(jnp.bfloat16), "expert", split_axis=0, concat_axis=2, tiled=True
        )
        .astype(own_columns.dtype)
        .reshape(q_tokens, -1)
    )
    attended = (hidden[0].astype(jnp.float32) + projected).astype(jnp.bfloat16)
    wide = attended.astype(jnp.float32)
    scale_rows = lax.rsqrt(jnp.mean(wide * wide, axis=1, keepdims=True) + 1e-06)
    normed = (wide * scale_rows * norm_gain.astype(jnp.float32)[None, :]).astype(jnp.bfloat16)
    experts = expert_in.shape[0] * expert_count
    capacity = 2 * q_tokens * TOP // experts
    positions = slot_positions(route_ids[0], experts, capacity)
    outgoing = place_rows(normed, positions, experts * capacity).reshape(experts, capacity, 1, -1)
    gathered = lax.all_gather(
        lax.all_to_all(outgoing, "expert", split_axis=0, concat_axis=0, tiled=True),
        "node",
        axis=2,
        tiled=True,
    )
    returned = lax.all_to_all(
        run_expert(gathered, expert_in, expert_out),
        "expert",
        split_axis=0,
        concat_axis=0,
        tiled=True,
    )
    returned = lax.psum_scatter(
        returned.astype(jnp.float32).astype(jnp.bfloat16), "node", scatter_dimension=2, tiled=True
    ).astype(jnp.float32)
    mixed = combine_rows(
        route_gates[0], positions, experts * capacity, returned.reshape(experts * capacity, -1)
    )
    moe_out = mixed.astype(jnp.bfloat16).reshape(1, q_tokens, -1)
    return (latent_out, attended.reshape(1, q_tokens, -1), moe_out)


def solution(mesh):
    in_specs = (
        P("expert", "node", None),
        P("expert", "node", None),
        P("expert", None, None),
        P("expert", "node", None),
        P("node", "expert", None),
        P("node", "expert"),
        P(),
        P("expert", "node", None),
        P("expert", "node", None),
        P("expert", None, None, "node"),
        P("expert", "node", None),
    )
    out_specs = (P("expert", "node", None), P("expert", "node", None), P("expert", "node", None))
    return jax.shard_map(shards, mesh=mesh, in_specs=in_specs, out_specs=out_specs, check_vma=False)
```

profile of v0, /device:TPU:6, one launch (start us, length us, event | category | flops | bytes accessed | tf_op | source)
XLA Modules:
  0.0 893.7 jit_solution(14069025622820199983)
XLA Ops:
  7.2 0.7 all-gather.5.cloned.1.call-update
  8.0 0.7 all-gather.7.cloned.1.call-update
  8.7 1.7 reshape_squeeze.6
  10.5 0.8 fusion.24
  11.4 82.6 %all-gather.5.cloned.1.call-done = bf16[1,2048,576]{1,2,0:T(8,128)(2,1)} async-done(((bf16[1,256,576]{1,2,0:T(8,128)(2,1)}), bf16[1,2048,576]{1,2,0:T(8,128)(2,1)}) %all-gather.5.cloned.1.call-update) | async-done | bytes 2359312 | tf_op jit(solution)/shard_map/all_gather | solution.py:86
  94.0 3.7 fusion.1
  97.7 1.3 fusion.3
  99.4 1.3 fusion.10
  101.3 20.5 %all_to_all.34 = bf16[4,8,8192]{2,0,1:T(4,128)(2,1)S(1)} all-to-all(bf16[4,8,8192]{2,0,1:T(4,128)(2,1)S(1)} %copy.45), channel_id=1, replica_groups=mesh['expert'=32,'node'=8] {'node'}, dimensions={1} | all-to-all | bytes 1048576 | tf_op jit(solution)/shard_map/all_to_all | solution.py:111
  122.2 36.9 %all-gather.7.cloned.1.call-done = bf16[16,512,128]{2,1,0:T(8,128)(2,1)} async-done(((bf16[16,16,128]{2,1,0:T(8,128)(2,1)}), bf16[16,512,128]{2,1,0:T(8,128)(2,1)}) %all-gather.7.cloned.1.call-update) | async-done | bytes 2097168 | tf_op jit(solution)/shard_map/all_gather | solution.py:117
  159.2 2.2 fusion.13
  162.1 66.0 %all-gather.9.cloned.1.call-done = bf16[1024,2048]{1,0:T(8,128)(2,1)} async-done(((bf16[32,2048]{1,0:T(8,128)(2,1)}), bf16[1024,2048]{1,0:T(8,128)(2,1)}) %all-gather.9.cloned.1.call-update) | async-done | bytes 4194320 | tf_op jit(solution)/shard_map/all_gather | solution.py:122
  228.1 3.6 convolution_convert_fusion.3
  232.2 1.2 copy.50
  233.9 83.7 %reduce-scatter.3.cloned.1.call-done = bf16[1,128,224]{1,2,0:T(8,128)(2,1)} async-done(((bf16[8,128,224]{1,2,0:T(8,128)(2,1)}), bf16[1,128,224]{1,2,0:T(8,128)(2,1)}) %reduce-scatter.3.cloned.1.call-update) | async-done | bytes 57360 | tf_op jit(solution)/shard_map/reduce_scatter | solution.py:131
  317.7 0.9 copy.51
  319.3 5.1 all-to-all-start.1
  324.5 6.0 all-to-all-done.1
  331.6 28.0 %all_to_all.35 = bf16[32,2,1,7168]{3,1,2,0:T(2,128)(2,1)S(1)} all-to-all(bf16[32,2,1,7168]{3,1,2,0:T(2,128)(2,1)S(1)} %bitcast.87), channel_id=1, replica_groups=mesh['expert'=32,'node'=8] {'expert'}, dimensions={0} | all-to-all | bytes 1835008 | tf_op jit(solution)/shard_map/all_to_all | solution.py:151
  359.7 1.1 copy.55
  361.0 7.4 copy.61
  368.4 146.8 %all-gather.11.cloned.1.call-done = bf16[32,2,8,7168]{3,0,1,2:T(8,128)(2,1)} async-done(((bf16[32,2,1,7168]{3,0,1,2:T(8,128)(2,1)}), bf16[32,2,8,7168]{3,0,1,2:T(8,128)(2,1)}) %all-gather.11.cloned.1.call-update) | async-done | bytes 7340048 | tf_op jit(solution)/shard_map/all_gather | solution.py:150
  515.2 10.2 %copy.56 = bf16[32,2,8,7168]{3,2,1,0:T(8,128)(2,1)} copy(bf16[32,2,8,7168]{3,0,1,2:T(8,128)(2,1)} %all-gather.11.cloned.1.call-done) | data formatting | bytes 14680064 | tf_op jit(solution)/shard_map/all_gather | solution.py:150
  525.4 6.3 fusion.45
  531.7 2.1 convolution_convert_fusion
  533.8 8.6 copy.57
  542.4 165.5 %all_to_all.36 = bf16[32,2,8,7168]{3,1,2,0:T(2,128)(2,1)S(1)} all-to-all(bf16[32,2,8,7168]{3,1,2,0:T(2,128)(2,1)S(1)} %copy.57), channel_id=1, replica_groups=mesh['expert'=32,'node'=8] {'expert'}, dimensions={0} | all-to-all | bytes 14680064 | tf_op jit(solution)/shard_map/all_to_all | solution.py:156
  707.9 7.0 copy.58
  715.7 1.2 reshape_reshape.6
  717.6 165.6 %reduce-scatter.5.cloned.1.call-done = bf16[32,2,1,7168]{3,0,1,2:T(8,128)(2,1)} async-done(((bf16[32,2,8,7168]{3,0,1,2:T(8,128)(2,1)}), bf16[32,2,1,7168]{3,0,1,2:T(8,128)(2,1)}) %reduce-scatter.5.cloned.1.call-update) | async-done | bytes 917520 | tf_op jit(solution)/shard_map/reduce_scatter | solution.py:163
  883.3 2.1 copy.59
  885.8 1.1 fusion
  (62 shorter events, 7.5 us)
Async XLA Ops:
  7.2 221.0 %copy-start = (bf16[2048,224]{0,1:T(8,128)(2,1)S(1)}, bf16[2048,224]{0,1:T(8,128)(2,1)}, u32[]{:S(2)}) copy-start(bf16[2048,224]{0,1:T(8,128)(2,1)} %param.16) | copy-start | bytes 2752516
  7.2 86.8 %all-gather.5.cloned.1.call-start = ((), (), s32[]{:S(2)}) async-start(), calls=%async_computation.6 | async-start | bytes 2654208 | tf_op jit(solution)/shard_map/all_gather | solution.py:86
  7.9 151.2 %all-gather.7.cloned.1.call-start = ((), (), s32[]{:S(2)}) async-start(), calls=%async_computation.7 | async-start | bytes 2162688 | tf_op jit(solution)/shard_map/all_gather | solution.py:117
  8.7 219.5 %all-gather.9.cloned.1.call-start = ((), (), s32[]{:S(2)}) async-start(), calls=%async_computation.8 | async-start | bytes 4325376 | tf_op jit(solution)/shard_map/all_gather | solution.py:122
  97.7 1.7 copy-start.4
  162.1 71.4 %copy-start.6 = (s32[1,4,8]{2,1,0:T(4,128)S(1)}, s32[1,4,8]{2,1,0:T(4,128)}, u32[]{:S(2)}) copy-start(s32[1,4,8]{2,1,0:T(4,128)} %param.18) | copy-start | bytes 388
  162.1 71.8 %copy-start.7 = (bf16[7168]{0:T(1024)(128)(2,1)S(1)}, bf16[7168]{0:T(1024)(128)(2,1)}, u32[]{:S(2)}) copy-start(bf16[7168]{0:T(1024)(128)(2,1)} %param.17) | copy-start | bytes 43012
  162.1 155.6 %reduce-scatter.3.cloned.1.call-start = ((), (), s32[]{:S(2)}) async-start(), calls=%async_computation.9 | async-start | bytes 516096 | tf_op jit(solution)/shard_map/reduce_scatter | solution.py:131
  231.7 98.9 %copy-start.5 = (bf16[1,4,7168]{2,1,0:T(4,128)(2,1)S(1)}, bf16[1,4,7168]{2,1,0:T(4,128)(2,1)}, u32[]{:S(2)}) copy-start(bf16[1,4,7168]{2,1,0:T(4,128)(2,1)} %param.14) | copy-start | bytes 172036
  319.3 11.2 %all-to-all-start.1 = ((bf16[32,4,224]{2,1,0:T(4,128)(2,1)}), bf16[32,4,224]{2,1,0:T(4,128)(2,1)S(1)}, u32[]{:S(2)}, u32[]{:S(2)}) async-start(bf16[32,4,224]{2,1,0:T(4,128)(2,1)} %convert_element_type.123), calls=%async_computation.2 | async-start | bytes 131072 | tf_op jit(solution)/shard_map/all_to_all | solution.py:136
  324.3 190.9 %all-gather.11.cloned.1.call-start = ((), (), s32[]{:S(2)}) async-start(), calls=%async_computation.10 | async-start | bytes 8257536 | tf_op jit(solution)/shard_map/all_gather | solution.py:150
  360.8 522.5 %reduce-scatter.5.cloned.1.call-start = ((), (), s32[]{:S(2)}) async-start(), calls=%async_computation.11 | async-start | bytes 8257536 | tf_op jit(solution)/shard_map/reduce_scatter | solution.py:163
  515.2 10.2 %copy-start.2 = (bf16[896,8,2,256]{3,1,2,0:T(8,128)(2,1)S(1)}, bf16[896,8,2,256]{3,1,2,0:T(8,128)(2,1)}, u32[]{:S(2)}) copy-start(bf16[896,8,2,256]{3,1,2,0:T(8,128)(2,1)} %copy.61) | copy-start | bytes 22020100
  525.4 6.3 copy-start.3
  714.9 0.7 copy-start.8
  714.9 171.9 %copy-start.1 = (bf16[2048,224]{0,1:T(8,128)(2,1)S(1)}, bf16[2048,224]{0,1:T(8,128)(2,1)}, u32[]{:S(2)}) copy-start(bf16[2048,224]{0,1:T(8,128)(2,1)} %param.16) | copy-start | bytes 2752516
Sparse Core Ops, SparseCore 0:
  10.5 83.4 all-gather.4
  95.8 63.3 all-gather.6
  162.2 65.9 all-gather.8
  233.5 84.0 reduce-scatter.2
  360.9 154.2 all-gather.10
  715.0 168.1 reduce-scatter.4
where the time goes:
time: 895 us; the launch traced here: 894 us
  waiting for transfers between devices  589 us (66%)
  blocking collectives  214 us (24%)
  local copies, waits for them, and re-layouts  46.4 us (5%)
  matrix products  21.6 us (2%)
  between operations  14.4 us (2%)
    reduce_scatter x1, waiting for transfers between devices, shards(): lax.psum_scatter(returned.astype(jnp.float32).astype(jnp.bfloat16), 'node...  166 us
    all_to_all x1, blocking collectives, shards(): lax.all_to_all(run_expert(gathered, expert_in, expert_out), 'expert', spl...  166 us
    all_gather x1, waiting for transfers between devices, shards(): lax.all_gather(lax.all_to_all(outgoing, 'expert', split_axis=0, concat_ax...  147 us
    reduce_scatter x1, waiting for transfers between devices, shards(): lax.psum_scatter(regrouped.astype(jnp.bfloat16), 'node', scatter_dimensio...  83.7 us
    all_gather x1, waiting for transfers between devices, shards(): keys = lax.all_gather(latent, 'node', axis=1, tiled=True)[0]  82.6 us
    all_gather x1, waiting for transfers between devices, shards(): lax.all_gather(head_vals, 'expert', axis=0, tiled=True)  66 us
    all_gather x1, waiting for transfers between devices, shards(): lax.all_gather(value_up, 'expert', axis=1, tiled=True)  36.9 us
    all_to_all x1, blocking collectives, shards(): lax.all_to_all(outgoing, 'expert', split_axis=0, concat_axis=0, tiled=True)  28 us
  transfers between devices with their start and end apart: 7, of which 7 were waited for; matrix products, arithmetic and copies ran while one was open for 2% of the time, Pallas kernels for 0%

commit v1 on v0

v1 whole, which is shorter than its diff:
```python
import jax
import jax.numpy as jnp
from jax import lax
from jax.sharding import Mesh
from jax.sharding import PartitionSpec as P

HEADS = 128
LAT = 512
ROPE = 64
VDIM = 128
BLK = 256
QROWS = 4
score_scale = 192.0 ** (-0.5)

E = ("zl", "x", "c")
N = ("y", "zh")
Z = ("zh", "zl")


def shift(value, axis, by, size):
    return lax.ppermute(value, axis, [(i, (i + by) % size) for i in range(size)])


def ring_gather(axis, own):
    half = own.shape[0] // 2
    back1 = shift(own, axis, 1, 4)
    back3 = shift(own, axis, 3, 4)
    low = shift(back1[:half], axis, 1, 4)
    high = shift(back3[half:], axis, 3, 4)
    return [own, back1, jnp.concatenate([low, high]), back3]


def ring_scatter(axis, parts):
    half = parts[2].shape[0] // 2
    low = shift(parts[2][:half].astype(jnp.bfloat16), axis, 3, 4)
    high = shift(parts[2][half:].astype(jnp.bfloat16), axis, 1, 4)
    send1 = jnp.concatenate([parts[1][:half] + low, parts[1][half:]]).astype(jnp.bfloat16)
    send3 = jnp.concatenate([parts[3][:half], parts[3][half:] + high]).astype(jnp.bfloat16)
    from1 = shift(send1, axis, 3, 4)
    from3 = shift(send3, axis, 1, 4)
    return parts[0] + from1 + from3


def backwards(value, axis, me, size):
    turned = jnp.flip(value, axis)
    return lax.dynamic_slice_in_dim(
        jnp.concatenate([turned, turned], axis), size - 1 - me, size, axis
    )


def shards(
    queries,
    latent,
    tile_mask,
    hidden,
    value_up,
    out_proj,
    norm_gain,
    route_ids,
    route_gates,
    expert_in,
    expert_out,
):
    width = LAT + ROPE
    y, zh = lax.axis_index("y"), lax.axis_index("zh")
    x, zl, c = lax.axis_index("x"), lax.axis_index("zl"), lax.axis_index("c")
    node = y * 2 + zh
    expert = (zl * 4 + x) * 2 + c
    tokens = queries.shape[1]
    model = hidden.shape[2]

    across = shift(latent[0], "zh", 1, 2)
    near = ring_gather("y", latent[0])
    far = ring_gather("y", across)
    keys = jnp.concatenate(near + far)

    maps = lax.all_gather(value_up, E, axis=1, tiled=True)
    proj = lax.all_gather(out_proj, ("x", "c"), axis=1, tiled=True)
    in_other = shift(expert_in[0], "c", 1, 2)
    out_other = shift(expert_out[0], "c", 1, 2)
    w_in = jnp.concatenate(
        [expert_in[0].reshape(model, -1), in_other.reshape(model, -1)], axis=1
    )
    w_out = jnp.concatenate([expert_out[0], out_other])
    n_experts = expert_in.shape[0] * 32
    hits = route_ids[0][:, :, None] == jnp.arange(n_experts, dtype=jnp.int32)
    dense = jnp.sum(jnp.where(hits, route_gates[0][:, :, None], 0.0), axis=1)
    table = lax.all_gather(dense, Z + ("x", "y"), axis=0, tiled=False)
    table = table.reshape(8, 4, 4, tokens, n_experts)
    table = jnp.concatenate(
        [
            lax.dynamic_slice_in_dim(table, expert, 1, 4),
            lax.dynamic_slice_in_dim(table, expert + 1 - 2 * c, 1, 4),
        ],
        axis=4,
    )
    table = backwards(backwards(table, 1, x, 4), 2, y, 4)
    gates1 = table[:4].transpose(2, 1, 0, 3, 4).reshape(4, -1, 2)
    gates2 = table[4:].transpose(1, 2, 0, 3, 4).reshape(4, -1, 2)

    q_rows = queries[0].reshape(tokens * HEADS, width)
    steps = jnp.arange(4, dtype=jnp.int32)
    y_back = lax.rem(y - steps + 4, 4)
    blocks = jnp.concatenate([y_back * 2 + zh, y_back * 2 + (1 - zh)])
    mask_row = lax.dynamic_slice_in_dim(tile_mask[0], node, 1, 0)[0]
    picked = jnp.sum(
        jnp.where(blocks[:, None] == jnp.arange(8, dtype=jnp.int32), mask_row[None, :], 0), axis=1
    )
    inside = jnp.arange(BLK, dtype=jnp.int32)
    q_inside = BLK - QROWS + jnp.arange(tokens, dtype=jnp.int32)
    k_position = blocks[:, None] * BLK + inside
    causal = k_position[None] <= (node * BLK + q_inside)[:, None, None]
    allowed = causal & (picked == 1)[None, :, None]
    count = keys.shape[0]
    allowed = jnp.broadcast_to(
        allowed.reshape(tokens, 1, count), (tokens, HEADS, count)
    ).reshape(tokens * HEADS, count)
    scores = jnp.dot(q_rows, keys.T, preferred_element_type=jnp.float32) * score_scale
    masked = jnp.where(allowed, scores, -1e30)
    top = jnp.max(masked, axis=1)
    weights = jnp.where(allowed, jnp.exp(masked - top[:, None]), 0.0)
    total = jnp.sum(weights, axis=1)
    summed = jnp.dot(
        weights.astype(jnp.bfloat16), keys[:, :LAT], preferred_element_type=jnp.float32
    )
    latent_rows = (summed / total[:, None]).astype(jnp.bfloat16).reshape(tokens, HEADS * LAT)

    heads_here = HEADS // 8
    swapped = lax.all_to_all(
        latent_rows.reshape(tokens, 8, heads_here * LAT), N, split_axis=1, concat_axis=0, tiled=True
    )
    lifted = jnp.einsum(
        "thl,hlv->thv",
        swapped.reshape(8 * tokens, heads_here, LAT),
        maps,
        preferred_element_type=jnp.float32,
    )
    head_vals = lifted.astype(jnp.bfloat16).reshape(8 * tokens, heads_here * VDIM)
    column_vals = lax.all_gather(head_vals, "zl", axis=0, tiled=True)
    partial = jnp.dot(column_vals, proj, preferred_element_type=jnp.float32).astype(jnp.bfloat16)
    shared = lax.all_to_all(
        partial.reshape(32, tokens, -1), ("zl",) + N, split_axis=0, concat_axis=0, tiled=True
    )
    shared = jnp.sum(shared.reshape(4, 8, tokens, -1).astype(jnp.float32), axis=1)
    projected = shared.transpose(1, 0, 2).reshape(tokens, model)
    attended = (hidden[0].astype(jnp.float32) + projected).astype(jnp.bfloat16)
    wide = attended.astype(jnp.float32)
    scale_rows = lax.rsqrt(jnp.mean(wide * wide, axis=1, keepdims=True) + 1e-06)
    normed = (wide * scale_rows * norm_gain.astype(jnp.float32)[None, :]).astype(jnp.bfloat16)

    copies = jnp.broadcast_to(normed[None], (8, tokens, model))
    along_z = lax.all_to_all(copies, Z, split_axis=0, concat_axis=0, tiled=True)
    rows1 = jnp.concatenate(ring_gather("x", along_z[:4].reshape(4 * tokens, model)))
    rows2 = jnp.concatenate(ring_gather("y", along_z[4:].reshape(4 * tokens, model)))
    parts1 = ring_gather("y", rows1)
    parts2 = ring_gather("x", rows2)

    def run_experts(rows, gate):
        both = jnp.dot(rows, w_in, preferred_element_type=jnp.float32)
        both = both.reshape(rows.shape[0], 2, 2, -1)
        act = jax.nn.silu(both[:, :, 0]) * both[:, :, 1] * gate[:, :, None]
        act = act.astype(jnp.bfloat16).reshape(rows.shape[0], -1)
        return jnp.dot(act, w_out, preferred_element_type=jnp.float32)

    done1, done2 = [], []
    for s in range(4):
        rows = jnp.concatenate([parts1[s], parts2[s]])
        out = run_experts(rows, jnp.concatenate([gates1[s], gates2[s]]))
        done1.append(out[: rows.shape[0] // 2])
        done2.append(out[rows.shape[0] // 2 :])

    sum1 = ring_scatter("y", done1)
    sum2 = ring_scatter("x", done2)
    sum1 = ring_scatter("x", jnp.split(sum1, 4))
    sum2 = ring_scatter("y", jnp.split(sum2, 4))
    pieces = jnp.concatenate([sum1, sum2]).astype(jnp.bfloat16).reshape(8, tokens, model)
    pieces = lax.all_to_all(pieces, Z, split_axis=0, concat_axis=0, tiled=True)
    mixed = jnp.sum(pieces.astype(jnp.float32), axis=0)

    return (
        latent_rows.reshape(1, tokens, HEADS * LAT),
        attended.reshape(1, tokens, model),
        mixed.astype(jnp.bfloat16).reshape(1, tokens, model),
    )


def solution(mesh):
    fine = Mesh(mesh.devices.reshape(4, 4, 2, 4, 2), ("zl", "x", "c", "y", "zh"))
    in_specs = (
        P(E, N, None),
        P(E, N, None),
        P(E, None, None),
        P(E, N, None),
        P(N, E, None),
        P(N, E),
        P(),
        P(E, N, None),
        P(E, N, None),
        P(E, None, None, N),
        P(E, N, None),
    )
    out_specs = (P(E, N, None),) * 3
    return jax.shard_map(shards, mesh=fine, in_specs=in_specs, out_specs=out_specs, check_vma=False)
```

time: 895 us -> 678 us (0.76)
  waiting for transfers between devices: 589 us -> 47.6 us
  blocking collectives: 214 us -> 347 us
  starting transfers between devices: 5.48 us -> 108 us
  local copies, waits for them, and re-layouts: 46.4 us -> 85.3 us
  matrix products: 21.6 us -> 56.8 us
    all_gather x0 -> x2, blocking collectives: none -> 347 us  [the longest x1 316 us: shards(): table = lax.all_gather(dense, Z + ('x', 'y'), axis=0, tiled=False)]
    all_gather x4 -> x2, waiting for transfers between devices: 332 us -> 0.02 us  [the longest x1 0.02 us: shards(): maps = lax.all_gather(value_up, E, axis=1, tiled=True)]
    reduce_scatter x2 -> x0, waiting for transfers between devices: 249 us -> none  [the longest x1 166 us: shards(): lax.psum_scatter(returned.astype(jnp.float32).astype(jnp.bfloat16), 'node...]
    all_to_all x3 -> x0, blocking collectives: 214 us -> none  [the longest x1 166 us: shards(): lax.all_to_all(run_expert(gathered, expert_in, expert_out), 'expert', spl...]
    ppermute x0 -> x43, starting transfers between devices: none -> 69.5 us  [shift(): lax.ppermute(value, axis, [(i, (i + by) % size) for i in range(size)])]
    unnamed x19 -> x85, local copies, waits for them, and re-layouts: 8.39 us -> 44.3 us
    ppermute x0 -> x43, waiting for transfers between devices: none -> 34.7 us  [shift(): lax.ppermute(value, axis, [(i, (i + by) % size) for i in range(size)])]
    dot_general x7 -> x10, matrix products: 16.6 us -> 51 us  [the longest x4 22.7 us: run_experts(): both = jnp.dot(rows, w_in, preferred_element_type=jnp.float32)]
  transfers between devices with their start and end apart: 7 -> 49, of which waited for: 7 -> 15; matrix products, arithmetic and copies ran while one was open for 2% -> 19% of each run, Pallas kernels for 0% -> 0%
where the time goes in v1:
time: 678 us; the launch traced here: 671 us
  blocking collectives  347 us (51%)
  starting transfers between devices  108 us (16%)
  local copies, waits for them, and re-layouts  85.3 us (13%)
  matrix products  56.8 us (8%)
  waiting for transfers between devices  47.6 us (7%)
  between operations  15.2 us (2%)
  other arithmetic  11.5 us (2%)
    all_gather x1, blocking collectives, shards(): table = lax.all_gather(dense, Z + ('x', 'y'), axis=0, tiled=False)  316 us
    ppermute x43, starting transfers between devices, shift(): lax.ppermute(value, axis, [(i, (i + by) % size) for i in range(size)])  69.5 us
    unnamed x85, local copies, waits for them, and re-layouts  44.3 us
    ppermute x43, waiting for transfers between devices, shift(): lax.ppermute(value, axis, [(i, (i + by) % size) for i in range(size)])  34.7 us
    all_gather x1, blocking collectives, shards(): column_vals = lax.all_gather(head_vals, 'zl', axis=0, tiled=True)  31 us
    dot_general x4, matrix products, run_experts(): both = jnp.dot(rows, w_in, preferred_element_type=jnp.float32)  22.7 us
    dot_general x4, matrix products, run_experts(): return jnp.dot(act, w_out, preferred_element_type=jnp.float32)  20.5 us
    all_to_all x1, starting transfers between devices, shards(): lax.all_to_all(partial.reshape(32, tokens, -1), ('zl',) + N, split_axis=0...  13.9 us
  transfers between devices with their start and end apart: 49, of which 15 were waited for; matrix products, arithmetic and copies ran while one was open for 19% of the time, Pallas kernels for 0%

profile of v1, /device:TPU:6, one launch (start us, length us, event | category | flops | bytes accessed | tf_op | source)
XLA Modules:
  0.0 671.2 jit_solution(11460571775760786744)
XLA Ops:
  12.0 7.2 %collective-permute-start.4 = (bf16[256,576]{0,1:T(8,128)(2,1)}, bf16[256,576]{0,1:T(8,128)(2,1)S(1)}, u32[]{:S(2)}, u32[]{:S(2)}) collective-permute-start(bf16[256,576]{0,1:T(8,128)(2,1)} %bitcast.157), channel_id=1, source_target_pairs={{0,1},{1,0},{2,3},{3,2},{4,5},{5,4},{6,7},{7,6},{8,9},{9,8},{10,11... | collective-permute-start | bytes 884744 | tf_op jit(solution)/shard_map/ppermute | solution.py:21
  26.1 6.5 collective-permute-done.4
  32.7 3.2 collective-permute-start.7
  42.4 3.5 collective-permute-start.8
  50.1 6.4 broadcast_in_dim.67
  56.5 4.1 fusion
  65.5 10.0 %all-to-all-start = ((bf16[4,8,8192]{2,0,1:T(4,128)(2,1)}), bf16[4,8,8192]{2,0,1:T(4,128)(2,1)S(1)}, u32[]{:S(2)}, u32[]{:S(2)}) async-start(bf16[4,8,8192]{2,0,1:T(4,128)(2,1)} %copy.64), calls=%async_computation | async-start | bytes 1048576 | tf_op jit(solution)/shard_map/all_to_all | solution.py:129
  75.7 316.0 %all-gather.1 = f32[128,4,32]{2,1,0:T(4,128)S(1)} all-gather(f32[1,4,32]{2,1,0:T(4,128)S(1)} %bitcast.174), channel_id=2, replica_groups=mesh['zl'=4,'x'=4,'c'=2,'y'=4,'zh'=2] {'zh','zl','x','y'}, dimensions={0}, use_global_device_ids=true | all-gather | bytes 66048 | tf_op jit(solution)/shard_map/all_gather | solution.py:88
  396.7 31.0 %all_gather.16 = bf16[128,2048]{1,0:T(8,128)(2,1)S(1)} all-gather(bf16[32,2048]{1,0:T(8,128)(2,1)S(1)} %bitcast.154), channel_id=1, replica_groups=mesh['zl'=4,'x'=4,'c'=2,'y'=4,'zh'=2] {'zl'}, dimensions={0}, use_global_device_ids=true | all-gather | bytes 655360 | tf_op jit(solution)/shard_map/all_gather | solution.py:139
  427.7 5.6 convolution_convert_fusion.1
  434.2 13.9 %all-to-all-start.1 = ((bf16[32,4,1792]{2,1,0:T(4,128)(2,1)}), bf16[32,4,1792]{2,1,0:T(4,128)(2,1)S(1)}, u32[]{:S(2)}, u32[]{:S(2)}) async-start(bf16[32,4,1792]{2,1,0:T(4,128)(2,1)} %reshape.193), calls=%async_computation.1 | async-start | bytes 917504 | tf_op jit(solution)/shard_map/all_to_all | solution.py:141
  449.4 7.4 %copy.82 = bf16[896,8,2,256]{3,1,2,0:T(8,128)(2,1)} copy(bf16[896,8,2,256]{3,2,1,0:T(2,128)(2,1)} %bitcast.135) | data formatting | bytes 14680064
  462.8 7.0 %all-to-all-start.2 = ((bf16[8,4,7168]{2,1,0:T(4,128)(2,1)}), bf16[8,4,7168]{2,1,0:T(4,128)(2,1)S(1)}, u32[]{:S(2)}, u32[]{:S(2)}) async-start(bf16[8,4,7168]{2,1,0:T(4,128)(2,1)} %broadcast_in_dim.71), calls=%async_computation.2 | async-start | bytes 917504 | tf_op jit(solution)/shard_map/all_to_all | solution.py:152
  469.7 6.7 constant_dynamic-update-slice_fusion.21
  476.4 7.4 %copy.83 = bf16[896,8,2,256]{3,1,2,0:T(8,128)(2,1)} copy(bf16[896,8,2,256]{3,2,1,0:T(2,128)(2,1)} %bitcast.36) | data formatting | bytes 14680064
  484.0 6.5 collective-permute-start.9
  494.6 3.3 collective-permute-start.10
  511.8 6.6 constant_dynamic-update-slice_fusion.20
  518.4 3.1 collective-permute-start.20
  525.8 7.4 %fusion.24 = f32[128,1024]{1,0:T(8,128)S(1)} fusion(bf16[7168,1024]{1,0:T(8,128)(2,1)} %constant_dynamic-update-slice_fusion.20, bf16[64,7168]{1,0:T(8,128)(2,1)S(1)} %collective-permute-done.25, bf16[64,7168]{1,0:T(8,128)(2,1)S(1)} %collective-permute-done.22), kind=kOutput, calls=%fused_computation.30 | convolution fusion | flops 1882718208 | bytes 17039360 | tf_op jit(solution)/shard_map/dot_general | solution.py:159
  539.5 3.7 collective-permute-start.24
  548.2 5.2 fusion.82
  556.0 4.5 fusion.12
  563.6 6.8 %fusion.83 = (bf16[128,7168]{1,0:T(8,128)(2,1)}, f32[128,7168]{1,0:T(8,128)}) fusion(bf16[256,7168]{1,0:T(8,128)(2,1)} %collective-permute-done.18, bf16[256,7168]{1,0:T(8,128)(2,1)} %bitcast.178, f32[128,512]{1,0:T(8,128)} %bitcast.161, f32[128,512]{1,0:T(8,128)S(1)} %bitcast.164, f32[128,512]{1,0:T(8,128)S(1)} %bitcast.166), kind=kOutput, calls=%fused_computation.183 | convolution fusion | flops 955580416 | bytes 13631488 | tf_op jit(solution)/shard_map/dot_general | solution.py:163
  570.5 8.6 %fusion.16 = f32[128,1024]{1,0:T(8,128)} fusion(bf16[7168,1024]{1,0:T(8,128)(2,1)} %constant_dynamic-update-slice_fusion.20, bf16[32,7168]{1,0:T(8,128)(2,1)} %collective-permute-done.26, bf16[32,7168]{1,0:T(8,128)(2,1)} %collective-permute-done.24, bf16[32,7168]{1,0:T(8,128)(2,1)} %collective-permute-done.23, bf16[32,7168]{1,0:T(8,128)(2,1)} %collective-permute-done.21), kind=kOutput, calls=%fused_computation.22 | convolution fusion | flops 1886388224 | bytes 17039360 | tf_op jit(solution)/shard_map/dot_general | solution.py:159
  582.3 4.6 convolution_convert_fusion
  587.4 3.2 collective-permute-start.27
  592.6 4.3 collective-permute-done.29
  611.4 3.9 fusion.46
  631.4 3.3 collective-permute-start.40
  643.4 7.3 %all-to-all-start.3 = ((bf16[8,4,7168]{2,1,0:T(4,128)(2,1)}), bf16[8,4,7168]{2,1,0:T(4,128)(2,1)S(1)}, u32[]{:S(2)}, u32[]{:S(2)}) async-start(bf16[8,4,7168]{2,1,0:T(4,128)(2,1)} %convert_element_type.177), calls=%async_computation.3 | async-start | bytes 917504 | tf_op jit(solution)/shard_map/all_to_all | solution.py:177
  651.9 11.4 %all-to-all-done.3 = bf16[8,4,7168]{2,1,0:T(4,128)(2,1)S(1)} async-done(((bf16[8,4,7168]{2,1,0:T(4,128)(2,1)}), bf16[8,4,7168]{2,1,0:T(4,128)(2,1)S(1)}, u32[]{:S(2)}, u32[]{:S(2)}) %all-to-all-start.3) | async-done | bytes 458784 | tf_op jit(solution)/shard_map/all_to_all | solution.py:177
  (278 shorter events, 126.3 us)
Async XLA Ops:
  7.2 387.2 %all-gather.5.cloned.1.call-start = ((), (), s32[]{:S(2)}) async-start(), calls=%async_computation.4 | async-start | bytes 2162688 | tf_op jit(solution)/shard_map/all_gather | solution.py:77
  7.9 419.8 %all-gather.7.cloned.1.call-start = ((), (), s32[]{:S(2)}) async-start(), calls=%async_computation.5 | async-start | bytes 8257536 | tf_op jit(solution)/shard_map/all_gather | solution.py:78
  8.7 11.1 %collective-permute-start = (bf16[256,576]{0,1:T(8,128)(2,1)}, bf16[256,576]{0,1:T(8,128)(2,1)S(1)}, u32[]{:S(2)}, u32[]{:S(2)}) collective-permute-start(bf16[256,576]{0,1:T(8,128)(2,1)} %bitcast.155), channel_id=1, source_target_pairs={{0,2},{2,4},{4,6},{6,0},{1,3},{3,5},{5,7},{7,1},{8,10},{10,12},{12... | collective-permute-start | bytes 884744 | tf_op jit(solution)/shard_map/ppermute | solution.py:21
  10.3 12.8 %collective-permute-start.2 = (bf16[256,576]{0,1:T(8,128)(2,1)}, bf16[256,576]{0,1:T(8,128)(2,1)S(1)}, u32[]{:S(2)}, u32[]{:S(2)}) collective-permute-start(bf16[256,576]{0,1:T(8,128)(2,1)} %bitcast.156), channel_id=1, source_target_pairs={{0,6},{2,0},{4,2},{6,4},{1,7},{3,1},{5,3},{7,5},{8,14},{10,8},{12,... | collective-permute-start | bytes 884744 | tf_op jit(solution)/shard_map/ppermute | solution.py:21
  12.0 20.7 %collective-permute-start.4 = (bf16[256,576]{0,1:T(8,128)(2,1)}, bf16[256,576]{0,1:T(8,128)(2,1)S(1)}, u32[]{:S(2)}, u32[]{:S(2)}) collective-permute-start(bf16[256,576]{0,1:T(8,128)(2,1)} %bitcast.157), channel_id=1, source_target_pairs={{0,1},{1,0},{2,3},{3,2},{4,5},{5,4},{6,7},{7,6},{8,9},{9,8},{10,11... | collective-permute-start | bytes 884744 | tf_op jit(solution)/shard_map/ppermute | solution.py:21
  19.2 457.2 %collective-permute-start.17 = (bf16[7168,2,256]{2,1,0:T(2,128)(2,1)}, bf16[7168,2,256]{2,1,0:T(2,128)(2,1)}, u32[]{:S(2)}, u32[]{:S(2)}) collective-permute-start(bf16[7168,2,256]{2,1,0:T(2,128)(2,1)} %bitcast.134), channel_id=1, source_target_pairs={{0,8},{8,0},{1,9},{9,1},{2,10},{10,2},{3,11},{11,3},{4,12},{12,4},... | collective-permute-start | bytes 22020104 | tf_op jit(solution)/shard_map/ppermute | solution.py:21
  19.8 16.9 %collective-permute-start.1 = (bf16[128,576]{0,1:T(8,128)(2,1)S(1)}, bf16[128,576]{0,1:T(8,128)(2,1)S(1)}, u32[]{:S(2)}, u32[]{:S(2)}) collective-permute-start(bf16[128,576]{0,1:T(8,128)(2,1)S(1)} %slice.290), channel_id=1, source_target_pairs={{0,2},{2,4},{4,6},{6,0},{1,3},{3,5},{5,7},{7,1},{8,10},{10,12},{12... | collective-permute-start | bytes 442376 | tf_op jit(solution)/shard_map/ppermute | solution.py:21
  23.2 14.2 %collective-permute-start.3 = (bf16[128,576]{0,1:T(8,128)(2,1)S(1)}, bf16[128,576]{0,1:T(8,128)(2,1)S(1)}, u32[]{:S(2)}, u32[]{:S(2)}) collective-permute-start(bf16[128,576]{0,1:T(8,128)(2,1)S(1)} %slice.291), channel_id=1, source_target_pairs={{0,6},{2,0},{4,2},{6,4},{1,7},{3,1},{5,3},{7,5},{8,14},{10,8},{12,... | collective-permute-start | bytes 442376 | tf_op jit(solution)/shard_map/ppermute | solution.py:21
  32.7 9.7 %collective-permute-start.7 = (bf16[256,576]{0,1:T(8,128)(2,1)S(1)}, bf16[256,576]{0,1:T(8,128)(2,1)S(1)}, u32[]{:S(2)}, u32[]{:S(2)}) collective-permute-start(bf16[256,576]{0,1:T(8,128)(2,1)S(1)} %collective-permute-done.4), channel_id=1, source_target_pairs={{0,6},{2,0},{4,2},{6,4},{1,7},{3,1},{5,3},{7,5},{8,14},{10,8},{12,... | collective-permute-start | bytes 884744 | tf_op jit(solution)/shard_map/ppermute | solution.py:21
  65.5 328.5 %all-to-all-start = ((bf16[4,8,8192]{2,0,1:T(4,128)(2,1)}), bf16[4,8,8192]{2,0,1:T(4,128)(2,1)S(1)}, u32[]{:S(2)}, u32[]{:S(2)}) async-start(bf16[4,8,8192]{2,0,1:T(4,128)(2,1)} %copy.64), calls=%async_computation | async-start | bytes 1048576 | tf_op jit(solution)/shard_map/all_to_all | solution.py:129
  75.5 472.7 %collective-permute-start.18 = (bf16[256,7168]{1,0:T(8,128)(2,1)}, bf16[256,7168]{1,0:T(8,128)(2,1)}, u32[]{:S(2)}, u32[]{:S(2)}) collective-permute-start(bf16[256,7168]{1,0:T(8,128)(2,1)} %bitcast.177), channel_id=1, source_target_pairs={{0,8},{8,0},{1,9},{9,1},{2,10},{10,2},{3,11},{11,3},{4,12},{12,4},... | collective-permute-start | bytes 11010056 | tf_op jit(solution)/shard_map/ppermute | solution.py:21
  434.2 26.6 %all-to-all-start.1 = ((bf16[32,4,1792]{2,1,0:T(4,128)(2,1)}), bf16[32,4,1792]{2,1,0:T(4,128)(2,1)S(1)}, u32[]{:S(2)}, u32[]{:S(2)}) async-start(bf16[32,4,1792]{2,1,0:T(4,128)(2,1)} %reshape.193), calls=%async_computation.1 | async-start | bytes 917504 | tf_op jit(solution)/shard_map/all_to_all | solution.py:141
  462.8 21.0 %all-to-all-start.2 = ((bf16[8,4,7168]{2,1,0:T(4,128)(2,1)}), bf16[8,4,7168]{2,1,0:T(4,128)(2,1)S(1)}, u32[]{:S(2)}, u32[]{:S(2)}) async-start(bf16[8,4,7168]{2,1,0:T(4,128)(2,1)} %broadcast_in_dim.71), calls=%async_computation.2 | async-start | bytes 917504 | tf_op jit(solution)/shard_map/all_to_all | solution.py:152
  484.0 10.6 %collective-permute-start.9 = (bf16[16,7168]{1,0:T(8,128)(2,1)S(1)}, bf16[16,7168]{1,0:T(8,128)(2,1)S(1)}, u32[]{:S(2)}, u32[]{:S(2)}) collective-permute-start(bf16[16,7168]{1,0:T(8,128)(2,1)S(1)} %reshape.195), channel_id=1, source_target_pairs={{0,16},{16,32},{32,48},{48,0},{1,17},{17,33},{33,49},{49,1},{2,18}... | collective-permute-start | bytes 688136 | tf_op jit(solution)/shard_map/ppermute | solution.py:21
  508.9 15.0 %collective-permute-start.25 = (bf16[64,7168]{1,0:T(8,128)(2,1)}, bf16[64,7168]{1,0:T(8,128)(2,1)S(1)}, u32[]{:S(2)}, u32[]{:S(2)}) collective-permute-start(bf16[64,7168]{1,0:T(8,128)(2,1)} %get-tuple-element.50), channel_id=1, source_target_pairs={{0,48},{16,0},{32,16},{48,32},{1,49},{17,1},{33,17},{49,33},{2,50}... | collective-permute-start | bytes 2752520 | tf_op jit(solution)/shard_map/ppermute | solution.py:21
  509.1 14.8 %collective-permute-start.22 = (bf16[64,7168]{1,0:T(8,128)(2,1)}, bf16[64,7168]{1,0:T(8,128)(2,1)S(1)}, u32[]{:S(2)}, u32[]{:S(2)}) collective-permute-start(bf16[64,7168]{1,0:T(8,128)(2,1)} %get-tuple-element.56), channel_id=1, source_target_pairs={{0,6},{2,0},{4,2},{6,4},{1,7},{3,1},{5,3},{7,5},{8,14},{10,8},{12,... | collective-permute-start | bytes 2752520 | tf_op jit(solution)/shard_map/ppermute | solution.py:21
  518.4 19.3 %collective-permute-start.20 = (bf16[64,7168]{1,0:T(8,128)(2,1)}, bf16[64,7168]{1,0:T(8,128)(2,1)}, u32[]{:S(2)}, u32[]{:S(2)}) collective-permute-start(bf16[64,7168]{1,0:T(8,128)(2,1)} %get-tuple-element.50), channel_id=1, source_target_pairs={{0,16},{16,32},{32,48},{48,0},{1,17},{17,33},{33,49},{49,1},{2,18}... | collective-permute-start | bytes 2752520 | tf_op jit(solution)/shard_map/ppermute | solution.py:21
  521.5 23.1 %collective-permute-start.19 = (bf16[64,7168]{1,0:T(8,128)(2,1)}, bf16[64,7168]{1,0:T(8,128)(2,1)}, u32[]{:S(2)}, u32[]{:S(2)}) collective-permute-start(bf16[64,7168]{1,0:T(8,128)(2,1)} %get-tuple-element.56), channel_id=1, source_target_pairs={{0,2},{2,4},{4,6},{6,0},{1,3},{3,5},{5,7},{7,1},{8,10},{10,12},{12... | collective-permute-start | bytes 2752520 | tf_op jit(solution)/shard_map/ppermute | solution.py:21
  536.2 34.3 %collective-permute-start.26 = (bf16[32,7168]{1,0:T(8,128)(2,1)}, bf16[32,7168]{1,0:T(8,128)(2,1)}, u32[]{:S(2)}, u32[]{:S(2)}) collective-permute-start(bf16[32,7168]{1,0:T(8,128)(2,1)} %slice.316), channel_id=1, source_target_pairs={{0,48},{16,0},{32,16},{48,32},{1,49},{17,1},{33,17},{49,33},{2,50}... | collective-permute-start | bytes 1376264 | tf_op jit(solution)/shard_map/ppermute | solution.py:21
  539.5 31.0 %collective-permute-start.24 = (bf16[32,7168]{1,0:T(8,128)(2,1)}, bf16[32,7168]{1,0:T(8,128)(2,1)}, u32[]{:S(2)}, u32[]{:S(2)}) collective-permute-start(bf16[32,7168]{1,0:T(8,128)(2,1)} %slice.315), channel_id=1, source_target_pairs={{0,16},{16,32},{32,48},{48,0},{1,17},{17,33},{33,49},{49,1},{2,18}... | collective-permute-start | bytes 1376264 | tf_op jit(solution)/shard_map/ppermute | solution.py:21
  544.0 26.5 %collective-permute-start.23 = (bf16[32,7168]{1,0:T(8,128)(2,1)}, bf16[32,7168]{1,0:T(8,128)(2,1)}, u32[]{:S(2)}, u32[]{:S(2)}) collective-permute-start(bf16[32,7168]{1,0:T(8,128)(2,1)} %slice.314), channel_id=1, source_target_pairs={{0,6},{2,0},{4,2},{6,4},{1,7},{3,1},{5,3},{7,5},{8,14},{10,8},{12,... | collective-permute-start | bytes 1376264 | tf_op jit(solution)/shard_map/ppermute | solution.py:21
  546.4 24.0 %collective-permute-start.21 = (bf16[32,7168]{1,0:T(8,128)(2,1)}, bf16[32,7168]{1,0:T(8,128)(2,1)}, u32[]{:S(2)}, u32[]{:S(2)}) collective-permute-start(bf16[32,7168]{1,0:T(8,128)(2,1)} %slice.313), channel_id=1, source_target_pairs={{0,2},{2,4},{4,6},{6,0},{1,3},{3,5},{5,7},{7,1},{8,10},{10,12},{12... | collective-permute-start | bytes 1376264 | tf_op jit(solution)/shard_map/ppermute | solution.py:21
  587.1 9.8 %collective-permute-start.29 = (bf16[32,7168]{1,0:T(8,128)(2,1)S(1)}, bf16[32,7168]{1,0:T(8,128)(2,1)S(1)}, u32[]{:S(2)}, u32[]{:S(2)}) collective-permute-start(bf16[32,7168]{1,0:T(8,128)(2,1)S(1)} %get-tuple-element.30), channel_id=1, source_target_pairs={{0,2},{2,4},{4,6},{6,0},{1,3},{3,5},{5,7},{7,1},{8,10},{10,12},{12... | collective-permute-start | bytes 1376264 | tf_op jit(solution)/shard_map/ppermute | solution.py:21
  587.2 9.7 %collective-permute-start.37 = (bf16[32,7168]{1,0:T(8,128)(2,1)S(1)}, bf16[32,7168]{1,0:T(8,128)(2,1)S(1)}, u32[]{:S(2)}, u32[]{:S(2)}) collective-permute-start(bf16[32,7168]{1,0:T(8,128)(2,1)S(1)} %get-tuple-element.28), channel_id=1, source_target_pairs={{0,16},{16,32},{32,48},{48,0},{1,17},{17,33},{33,49},{49,1},{2,18}... | collective-permute-start | bytes 1376264 | tf_op jit(solution)/shard_map/ppermute | solution.py:21
  587.4 10.7 %collective-permute-start.27 = (bf16[32,7168]{1,0:T(8,128)(2,1)S(1)}, bf16[32,7168]{1,0:T(8,128)(2,1)S(1)}, u32[]{:S(2)}, u32[]{:S(2)}) collective-permute-start(bf16[32,7168]{1,0:T(8,128)(2,1)S(1)} %get-tuple-element.27), channel_id=1, source_target_pairs={{0,6},{2,0},{4,2},{6,4},{1,7},{3,1},{5,3},{7,5},{8,14},{10,8},{12,... | collective-permute-start | bytes 1376264 | tf_op jit(solution)/shard_map/ppermute | solution.py:21
  590.6 9.7 %collective-permute-start.35 = (bf16[32,7168]{1,0:T(8,128)(2,1)S(1)}, bf16[32,7168]{1,0:T(8,128)(2,1)S(1)}, u32[]{:S(2)}, u32[]{:S(2)}) collective-permute-start(bf16[32,7168]{1,0:T(8,128)(2,1)S(1)} %get-tuple-element.29), channel_id=1, source_target_pairs={{0,48},{16,0},{32,16},{48,32},{1,49},{17,1},{33,17},{49,33},{2,50}... | collective-permute-start | bytes 1376264 | tf_op jit(solution)/shard_map/ppermute | solution.py:21
  598.1 17.3 %collective-permute-start.30 = (bf16[64,7168]{1,0:T(8,128)(2,1)}, bf16[64,7168]{1,0:T(8,128)(2,1)}, u32[]{:S(2)}, u32[]{:S(2)}) collective-permute-start(bf16[64,7168]{1,0:T(8,128)(2,1)} %pad_maximum_fusion.2), channel_id=1, source_target_pairs={{0,2},{2,4},{4,6},{6,0},{1,3},{3,5},{5,7},{7,1},{8,10},{10,12},{12... | collective-permute-start | bytes 2752520 | tf_op jit(solution)/shard_map/ppermute | solution.py:21
  601.4 13.9 %collective-permute-start.28 = (bf16[64,7168]{1,0:T(8,128)(2,1)}, bf16[64,7168]{1,0:T(8,128)(2,1)}, u32[]{:S(2)}, u32[]{:S(2)}) collective-permute-start(bf16[64,7168]{1,0:T(8,128)(2,1)} %pad_maximum_fusion.1), channel_id=1, source_target_pairs={{0,6},{2,0},{4,2},{6,4},{1,7},{3,1},{5,3},{7,5},{8,14},{10,8},{12,... | collective-permute-start | bytes 2752520 | tf_op jit(solution)/shard_map/ppermute | solution.py:21
  604.1 13.7 %collective-permute-start.38 = (bf16[64,7168]{1,0:T(8,128)(2,1)}, bf16[64,7168]{1,0:T(8,128)(2,1)}, u32[]{:S(2)}, u32[]{:S(2)}) collective-permute-start(bf16[64,7168]{1,0:T(8,128)(2,1)} %pad_maximum_fusion.4), channel_id=1, source_target_pairs={{0,16},{16,32},{32,48},{48,0},{1,17},{17,33},{33,49},{49,1},{2,18}... | collective-permute-start | bytes 2752520 | tf_op jit(solution)/shard_map/ppermute | solution.py:21
  605.6 14.9 %collective-permute-start.36 = (bf16[64,7168]{1,0:T(8,128)(2,1)}, bf16[64,7168]{1,0:T(8,128)(2,1)}, u32[]{:S(2)}, u32[]{:S(2)}) collective-permute-start(bf16[64,7168]{1,0:T(8,128)(2,1)} %pad_maximum_fusion.3), channel_id=1, source_target_pairs={{0,48},{16,0},{32,16},{48,32},{1,49},{17,1},{33,17},{49,33},{2,50}... | collective-permute-start | bytes 2752520 | tf_op jit(solution)/shard_map/ppermute | solution.py:21
  625.5 9.1 %collective-permute-start.31 = (bf16[8,7168]{1,0:T(8,128)(2,1)S(1)}, bf16[8,7168]{1,0:T(8,128)(2,1)S(1)}, u32[]{:S(2)}, u32[]{:S(2)}) collective-permute-start(bf16[8,7168]{1,0:T(8,128)(2,1)S(1)} %get-tuple-element.37), channel_id=1, source_target_pairs={{0,48},{16,0},{32,16},{48,32},{1,49},{17,1},{33,17},{49,33},{2,50}... | collective-permute-start | bytes 344072 | tf_op jit(solution)/shard_map/ppermute | solution.py:21
  643.4 19.9 %all-to-all-start.3 = ((bf16[8,4,7168]{2,1,0:T(4,128)(2,1)}), bf16[8,4,7168]{2,1,0:T(4,128)(2,1)S(1)}, u32[]{:S(2)}, u32[]{:S(2)}) async-start(bf16[8,4,7168]{2,1,0:T(4,128)(2,1)} %convert_element_type.177), calls=%async_computation.3 | async-start | bytes 917504 | tf_op jit(solution)/shard_map/all_to_all | solution.py:177
  (41 other events, 371.0 us)
Sparse Core Ops, SparseCore 0:
  9.8 73.0 all-gather.4
  84.8 45.8 all-gather.6
